TPU v7x, 512 devices: a whole 4x8x8 slice. The times are simulated.
512 devices in a mesh: gx: 16 (over z, core), gy: 8 (over y), gz: 4 (over x).
Axes of the slice: x: 4, y: 8, z: 8, core: 2. Of those that a mesh axis runs over, the one named last changes fastest.
Arguments:
- start: float32 [4, 80, 256, 512], P(None, 'gx', 'gy', 'gz'), may hold values from -6 to 6
- rhs_block: float32 [4, 80, 256, 512], P(None, 'gx', 'gy', 'gz'), may hold values from -6 to 6
- coefficients: float32 [4, 80, 256, 512], P(None, 'gx', 'gy', 'gz'), may hold values from 0.5 to 2
Outputs:
- solution: float32 [4, 80, 256, 512], P(None, 'gx', 'gy', 'gz')
All inputs are finite; a program needn't handle non-finite values.
Results may differ from a plain program's by a relative error of at most 0.0003.
Values sent between devices are 32-bit elements; how exact they have to be, the bound alone decides.
A program may use at most 192 MiB of HBM per device.

v0:
```python
import jax
import jax.numpy as jnp
from jax import lax
from jax.sharding import PartitionSpec as P

S = 4
basis_shift = 8.75
basis_scale = 4.0


def padded(block, sides, width):
    for axis, dim in sides:
        count = lax.axis_size(axis)
        forward = [(i, i + 1) for i in range(count - 1)]
        backward = [(target, source) for source, target in forward]
        low = lax.ppermute(
            lax.slice_in_dim(block, block.shape[dim] - width, None, axis=dim), axis, forward
        )
        high = lax.ppermute(lax.slice_in_dim(block, 0, width, axis=dim), axis, backward)
        block = jnp.concatenate([low, block, high], axis=dim)
    return block


def stencil(field, coefs):
    center = field[:, 1:-1, 1:-1, 1:-1]
    result = coefs[0, 1:-1, 1:-1, 1:-1] * center
    result = result + coefs[1, 1:-1, 1:-1, 1:-1] * (center - field[:, 2:, 1:-1, 1:-1])
    result = result + coefs[1, :-2, 1:-1, 1:-1] * (center - field[:, :-2, 1:-1, 1:-1])
    result = result + coefs[2, 1:-1, 1:-1, 1:-1] * (center - field[:, 1:-1, 2:, 1:-1])
    result = result + coefs[2, 1:-1, :-2, 1:-1] * (center - field[:, 1:-1, :-2, 1:-1])
    result = result + coefs[3, 1:-1, 1:-1, 1:-1] * (center - field[:, 1:-1, 1:-1, 2:])
    result = result + coefs[3, 1:-1, 1:-1, :-2] * (center - field[:, 1:-1, 1:-1, :-2])
    return result


def reflect_rows(tall):
    count = tall.shape[0]
    entries = tall.shape[1]
    position = jnp.arange(entries)
    for j in range(count):
        column = jnp.where(position >= j, tall[j], 0.0)
        length = jnp.sqrt(jnp.sum(column * column))
        leading = tall[j, j]
        mirror = -jnp.where(leading >= 0, 1.0, -1.0) * length
        vector = column - mirror * (position == j).astype(jnp.float32)
        weight = jnp.sum(vector * vector)
        project = jnp.dot(tall, vector, precision=lax.Precision.HIGHEST) / weight
        tall = tall - 2.0 * project[:, None] * vector[None, :]
    factor = tall.T
    flip_sign = jnp.where(jnp.diagonal(factor) >= 0, 1.0, -1.0)
    return jnp.triu(factor * flip_sign[:, None])


def back_solve(triangle, values):
    count = triangle.shape[0]
    answer = [None] * count
    for i in reversed(range(count)):
        partial_sum = values[i]
        for j in range(i + 1, count):
            partial_sum = partial_sum - triangle[i, j] * answer[j]
        answer[i] = partial_sum / triangle[i, i]
    return jnp.stack(answer)


def least_squares(upper, nrhs):
    total = upper.shape[0]
    kept = total - nrhs
    rows = jnp.arange(total)[:, None]
    cols = jnp.arange(kept)[None, :]
    shifts = basis_shift * (rows == cols).astype(jnp.float32) + basis_scale * (
        rows == cols + nrhs
    ).astype(jnp.float32)
    mixed = jnp.dot(upper, shifts, precision=lax.Precision.HIGHEST)
    joined = jnp.concatenate([mixed, upper[:, :nrhs]], axis=1)
    reduced = reflect_rows(joined.T)
    return back_solve(reduced[:kept, :kept], reduced[:kept, kept:])


def local(start, rhs_block, coefficients):
    nrhs = start.shape[0]
    guess_ext, coef_ext = (
        padded(start, (("gx", 1), ("gy", 2), ("gz", 3)), 1),
        padded(coefficients, (("gx", 1), ("gy", 2), ("gz", 3)), 1),
    )
    blocks = [rhs_block - stencil(guess_ext, coef_ext)]
    for step in range(S):
        before = blocks[-1]
        widened = padded(before, (("gx", 1), ("gy", 2), ("gz", 3)), 1)
        blocks.append((stencil(widened, coef_ext) - basis_shift * before) / basis_scale)
    tall = jnp.stack(blocks).reshape(len(blocks) * nrhs, -1)
    local_gram = jnp.dot(tall, tall.T, precision=lax.Precision.HIGHEST)
    gram = lax.psum(local_gram, ("gx", "gy", "gz"))
    upper = jnp.linalg.cholesky(gram).T
    weights = least_squares(upper, nrhs)
    kept = tall.shape[0] - nrhs
    update = jnp.dot(weights.T, tall[:kept], precision=lax.Precision.HIGHEST)
    return start + update.reshape(start.shape)


def solution(mesh):
    placed = (P(None, "gx", "gy", "gz"), P(None, "gx", "gy", "gz"), P(None, "gx", "gy", "gz"))
    return jax.shard_map(
        local, mesh=mesh, in_specs=placed, out_specs=P(None, "gx", "gy", "gz"), check_vma=False
    )
```

profile of v0, /device:TPU:1, one launch (start us, length us, event | category | flops | bytes accessed | tf_op | source)
XLA Modules:
  0.0 541.6 jit_solution(3785583033890651326)
XLA Ops:
  0.9 5.5 %collective-permute-start.1 = (f32[4,1,32,128]{3,2,1,0:T(8,128)S(1)}, f32[4,1,32,128]{3,2,1,0:T(8,128)S(1)}, u32[]{:S(2)}, u32[]{:S(2)}) collective-permute-start(f32[4,1,32,128]{3,2,1,0:T(8,128)S(1)} %get-tuple-element.80), channel_id=1, source_target_pairs={{0,32},{32,64},{64,96},{96,128},{128,160},{160,192},{192,224},{224... | collective-permute-start | bytes 196616 | tf_op jit(solution)/shard_map/ppermute | solution.py:16
  6.5 4.7 collective-permute-start.4
  12.1 1.9 collective-permute-start.2
  14.0 2.4 collective-permute-start
  24.1 5.2 collective-permute-start.6
  31.2 2.0 copy.479
  33.2 1.9 copy.481
  36.0 3.1 collective-permute-start.9
  45.9 4.0 collective-permute-start.10
  50.8 2.4 fusion.42
  56.7 2.2 constant_dynamic-update-slice_fusion.9
  58.9 1.9 collective-permute-start.11
  60.8 5.3 collective-permute-start.12
  68.8 4.0 collective-permute-start.14
  78.9 4.0 collective-permute-start.16
  88.8 1.9 collective-permute-start.17
  90.7 6.2 %collective-permute-start.18 = (f32[4,1,32,128]{3,2,1,0:T(8,128)S(1)}, f32[4,1,32,128]{3,2,1,0:T(8,128)S(1)}, u32[]{:S(2)}, u32[]{:S(2)}) collective-permute-start(f32[4,1,32,128]{3,2,1,0:T(8,128)S(1)} %get-tuple-element.70), channel_id=1, source_target_pairs={{0,32},{32,64},{64,96},{96,128},{128,160},{160,192},{192,224},{224... | collective-permute-start | bytes 196616 | tf_op jit(solution)/shard_map/ppermute | solution.py:16
  99.6 4.5 collective-permute-start.20
  107.2 4.5 collective-permute-start.22
  117.3 5.6 %collective-permute-start.24 = (f32[4,1,32,128]{3,2,1,0:T(8,128)S(1)}, f32[4,1,32,128]{3,2,1,0:T(8,128)S(1)}, u32[]{:S(2)}, u32[]{:S(2)}) collective-permute-start(f32[4,1,32,128]{3,2,1,0:T(8,128)S(1)} %get-tuple-element.68), channel_id=1, source_target_pairs={{0,32},{32,64},{64,96},{96,128},{128,160},{160,192},{192,224},{224... | collective-permute-start | bytes 196616 | tf_op jit(solution)/shard_map/ppermute | solution.py:16
  125.5 4.5 collective-permute-start.26
  133.1 4.5 collective-permute-start.28
  139.3 1.9 collective-permute-start.29
  141.2 6.0 %collective-permute-start.30 = (f32[4,1,32,128]{3,2,1,0:T(8,128)S(1)}, f32[4,1,32,128]{3,2,1,0:T(8,128)S(1)}, u32[]{:S(2)}, u32[]{:S(2)}) collective-permute-start(f32[4,1,32,128]{3,2,1,0:T(8,128)S(1)} %get-tuple-element.62), channel_id=1, source_target_pairs={{0,32},{32,64},{64,96},{96,128},{128,160},{160,192},{192,224},{224... | collective-permute-start | bytes 196616 | tf_op jit(solution)/shard_map/ppermute | solution.py:16
  149.9 5.5 %collective-permute-start.32 = (f32[4,7,1,128]{3,0,2,1:T(4,128)S(1)}, f32[4,7,1,128]{3,0,2,1:T(4,128)S(1)}, u32[]{:S(2)}, u32[]{:S(2)}) collective-permute-start(f32[4,7,1,128]{3,0,2,1:T(4,128)S(1)} %copy.517), channel_id=1, source_target_pairs={{0,4},{4,8},{8,12},{12,16},{16,20},{20,24},{24,28},{1,5},{5,9},{9,... | collective-permute-start | bytes 43016 | tf_op jit(solution)/shard_map/ppermute | solution.py:16
  159.0 5.1 collective-permute-start.34
  171.2 2.2 fusion.49
  175.2 2.1 fusion.311
  177.3 116.5 %psum.7 = f32[20,20]{0,1:T(8,128)S(1)} all-reduce(f32[20,20]{0,1:T(8,128)S(1)} %fusion.311), channel_id=1, replica_groups=mesh['gx'=16,'gy'=8,'gz'=4] {'gx','gy','gz'}, use_global_device_ids=true, to_apply=%region_0.0 | all-reduce | flops 400 | bytes 3200 | tf_op jit(solution)/shard_map/psum | solution.py:92
  395.1 65.5 %subtract_divide_fusion = (f32[1,4]{1,0:T(1,128)S(1)}, f32[1,4]{1,0:T(1,128)S(1)}, f32[1,4]{1,0:T(1,128)S(1)}, f32[1,4]{1,0:T(1,128)S(1)}, f32[1,4]{1,0:T(1,128)...) fusion(f32[20,20]{1,0:T(8,128)S(1)} %multiply_select_fusion, ...), kind=kLoop, calls=%fused_computation.602 | loop fusion | flops 784 | bytes 884 | tf_op jit(solution)/shard_map/div | solution.py:61
  461.0 57.8 %fusion.191 = (f32[4]{0:T(128)S(1)}, f32[4]{0:T(128)S(1)}, f32[4]{0:T(128)S(1)}, f32[4]{0:T(128)S(1)}, f32[4]{0:T(128)S(1)}, /*index=5*/f32[4]{0:T(128)S(1)}, f3...) fusion(f32[20,20]{1,0:T(8,128)S(1)} %multiply_select_fusion, f32[1,4]{1,0:T(1,128)S(1)} %get-tuple-element.16, ...), kind=kLoop, calls=%fused_computation.504 | loop fusion | flops 704 | bytes 756 | tf_op jit(solution)/shard_map/div | solution.py:61
  518.8 19.3 %fusion.244 = (f32[1,4]{1,0:T(1,128)S(1)}, f32[4]{0:T(128)S(1)}) fusion(f32[1,4]{1,0:T(1,128)S(1)} %get-tuple-element.19, f32[1,4]{1,0:T(1,128)S(1)} %get-tuple-element.18, f32[1,4]{1,0:T(1,128)S(1)} %get-tuple-element.17, f32[1,4]{1,0:T(1,128)S(1)} %get-tuple-element.16, f32[4]{0:T(128)S(1)} %get-tuple-element.31, f32[4]{0:T(128)S(1)} %get-tuple-element.30, ...), kind=kLoop, calls=%fused_computation.656 | loop fusion | flops 240 | bytes 412 | tf_op jit(solution)/shard_map/stack | solution.py:62
  (370 shorter events, 147.8 us)
Async XLA Ops:
  0.9 15.5 %collective-permute-start.1 = (f32[4,1,32,128]{3,2,1,0:T(8,128)S(1)}, f32[4,1,32,128]{3,2,1,0:T(8,128)S(1)}, u32[]{:S(2)}, u32[]{:S(2)}) collective-permute-start(f32[4,1,32,128]{3,2,1,0:T(8,128)S(1)} %get-tuple-element.80), channel_id=1, source_target_pairs={{0,32},{32,64},{64,96},{96,128},{128,160},{160,192},{192,224},{224... | collective-permute-start | bytes 196616 | tf_op jit(solution)/shard_map/ppermute | solution.py:16
  6.5 11.0 %collective-permute-start.4 = (f32[4,1,32,128]{3,2,1,0:T(8,128)S(1)}, f32[4,1,32,128]{3,2,1,0:T(8,128)S(1)}, u32[]{:S(2)}, u32[]{:S(2)}) collective-permute-start(f32[4,1,32,128]{3,2,1,0:T(8,128)S(1)} %get-tuple-element.79), channel_id=1, source_target_pairs={{32,0},{64,32},{96,64},{128,96},{160,128},{192,160},{224,192},{256... | collective-permute-start | bytes 196616 | tf_op jit(solution)/shard_map/ppermute | solution.py:19
  12.1 9.3 %collective-permute-start.2 = (f32[4,1,32,128]{3,2,1,0:T(8,128)S(1)}, f32[4,1,32,128]{3,2,1,0:T(8,128)S(1)}, u32[]{:S(2)}, u32[]{:S(2)}) collective-permute-start(f32[4,1,32,128]{3,2,1,0:T(8,128)S(1)} %get-tuple-element.82), channel_id=1, source_target_pairs={{0,32},{32,64},{64,96},{96,128},{128,160},{160,192},{192,224},{224... | collective-permute-start | bytes 196616 | tf_op jit(solution)/shard_map/ppermute | solution.py:16
  14.0 7.5 %collective-permute-start = (f32[4,1,32,128]{3,2,1,0:T(8,128)S(1)}, f32[4,1,32,128]{3,2,1,0:T(8,128)S(1)}, u32[]{:S(2)}, u32[]{:S(2)}) collective-permute-start(f32[4,1,32,128]{3,2,1,0:T(8,128)S(1)} %get-tuple-element.81), channel_id=1, source_target_pairs={{32,0},{64,32},{96,64},{128,96},{160,128},{192,160},{224,192},{256... | collective-permute-start | bytes 196616 | tf_op jit(solution)/shard_map/ppermute | solution.py:19
  18.4 12.8 %collective-permute-start.5 = (f32[4,7,1,128]{3,1,2,0:T(8,128)}, f32[4,7,1,128]{3,1,2,0:T(8,128)S(1)}, u32[]{:S(2)}, u32[]{:S(2)}) collective-permute-start(f32[4,7,1,128]{3,1,2,0:T(8,128)} %get-tuple-element.50), channel_id=1, source_target_pairs={{0,4},{4,8},{8,12},{12,16},{16,20},{20,24},{24,28},{1,5},{5,9},{9,... | collective-permute-start | bytes 43016 | tf_op jit(solution)/shard_map/ppermute | solution.py:16
  20.1 13.1 %collective-permute-start.8 = (f32[4,7,1,128]{3,1,2,0:T(8,128)}, f32[4,7,1,128]{3,1,2,0:T(8,128)S(1)}, u32[]{:S(2)}, u32[]{:S(2)}) collective-permute-start(f32[4,7,1,128]{3,1,2,0:T(8,128)} %get-tuple-element.51), channel_id=1, source_target_pairs={{4,0},{8,4},{12,8},{16,12},{20,16},{24,20},{28,24},{5,1},{9,5},{13... | collective-permute-start | bytes 43016 | tf_op jit(solution)/shard_map/ppermute | solution.py:19
  22.2 16.9 %collective-permute-start.3 = (f32[4,7,1,128]{3,0,2,1:T(4,128)}, f32[4,7,1,128]{3,0,2,1:T(4,128)}, u32[]{:S(2)}, u32[]{:S(2)}) collective-permute-start(f32[4,7,1,128]{3,0,2,1:T(4,128)} %copy.550), channel_id=1, source_target_pairs={{4,0},{8,4},{12,8},{16,12},{20,16},{24,20},{28,24},{5,1},{9,5},{13... | collective-permute-start | bytes 43016 | tf_op jit(solution)/shard_map/ppermute | solution.py:19
  24.1 15.8 %collective-permute-start.6 = (f32[4,7,1,128]{3,0,2,1:T(4,128)}, f32[4,7,1,128]{3,0,2,1:T(4,128)}, u32[]{:S(2)}, u32[]{:S(2)}) collective-permute-start(f32[4,7,1,128]{3,0,2,1:T(4,128)} %copy.551), channel_id=1, source_target_pairs={{0,4},{4,8},{8,12},{12,16},{16,20},{20,24},{24,28},{1,5},{5,9},{9,... | collective-permute-start | bytes 43016 | tf_op jit(solution)/shard_map/ppermute | solution.py:16
  36.0 14.8 %collective-permute-start.9 = (f32[4,7,34,1]{2,1,3,0:T(8,128)S(1)}, f32[4,7,34,1]{2,1,3,0:T(8,128)S(1)}, u32[]{:S(2)}, u32[]{:S(2)}) collective-permute-start(f32[4,7,34,1]{2,1,3,0:T(8,128)S(1)} %pad_maximum_fusion.93), channel_id=1, source_target_pairs={{0,1},{1,2},{2,3},{4,5},{5,6},{6,7},{8,9},{9,10},{10,11},{12,13},{... | collective-permute-start | bytes 11432 | tf_op jit(solution)/shard_map/ppermute | solution.py:16
  43.2 11.2 %collective-permute-start.7 = (f32[4,7,34,1]{2,0,3,1:T(4,128)S(1)}, f32[4,7,34,1]{2,0,3,1:T(4,128)S(1)}, u32[]{:S(2)}, u32[]{:S(2)}) collective-permute-start(f32[4,7,34,1]{2,0,3,1:T(4,128)S(1)} %copy.476), channel_id=1, source_target_pairs={{1,0},{2,1},{3,2},{5,4},{6,5},{7,6},{9,8},{10,9},{11,10},{13,12},{... | collective-permute-start | bytes 11432 | tf_op jit(solution)/shard_map/ppermute | solution.py:19
  45.9 9.7 %collective-permute-start.10 = (f32[4,7,34,1]{2,0,3,1:T(4,128)S(1)}, f32[4,7,34,1]{2,0,3,1:T(4,128)S(1)}, u32[]{:S(2)}, u32[]{:S(2)}) collective-permute-start(f32[4,7,34,1]{2,0,3,1:T(4,128)S(1)} %copy.483), channel_id=1, source_target_pairs={{0,1},{1,2},{2,3},{4,5},{5,6},{6,7},{8,9},{9,10},{10,11},{12,13},{... | collective-permute-start | bytes 11432 | tf_op jit(solution)/shard_map/ppermute | solution.py:16
  58.9 7.3 %collective-permute-start.11 = (f32[4,1,32,128]{3,2,1,0:T(8,128)S(1)}, f32[4,1,32,128]{3,2,1,0:T(8,128)S(1)}, u32[]{:S(2)}, u32[]{:S(2)}) collective-permute-start(f32[4,1,32,128]{3,2,1,0:T(8,128)S(1)} %get-tuple-element.73), channel_id=1, source_target_pairs={{32,0},{64,32},{96,64},{128,96},{160,128},{192,160},{224,192},{256... | collective-permute-start | bytes 196616 | tf_op jit(solution)/shard_map/ppermute | solution.py:19
  60.8 6.6 %collective-permute-start.12 = (f32[4,1,32,128]{3,2,1,0:T(8,128)S(1)}, f32[4,1,32,128]{3,2,1,0:T(8,128)S(1)}, u32[]{:S(2)}, u32[]{:S(2)}) collective-permute-start(f32[4,1,32,128]{3,2,1,0:T(8,128)S(1)} %get-tuple-element.72), channel_id=1, source_target_pairs={{0,32},{32,64},{64,96},{96,128},{128,160},{160,192},{192,224},{224... | collective-permute-start | bytes 196616 | tf_op jit(solution)/shard_map/ppermute | solution.py:16
  76.2 6.6 %collective-permute-start.15 = (f32[4,7,34,1]{2,0,3,1:T(4,128)S(1)}, f32[4,7,34,1]{2,0,3,1:T(4,128)S(1)}, u32[]{:S(2)}, u32[]{:S(2)}) collective-permute-start(f32[4,7,34,1]{2,0,3,1:T(4,128)S(1)} %copy.491), channel_id=1, source_target_pairs={{1,0},{2,1},{3,2},{5,4},{6,5},{7,6},{9,8},{10,9},{11,10},{13,12},{... | collective-permute-start | bytes 11432 | tf_op jit(solution)/shard_map/ppermute | solution.py:19
  88.8 8.2 %collective-permute-start.17 = (f32[4,1,32,128]{3,2,1,0:T(8,128)S(1)}, f32[4,1,32,128]{3,2,1,0:T(8,128)S(1)}, u32[]{:S(2)}, u32[]{:S(2)}) collective-permute-start(f32[4,1,32,128]{3,2,1,0:T(8,128)S(1)} %get-tuple-element.71), channel_id=1, source_target_pairs={{32,0},{64,32},{96,64},{128,96},{160,128},{192,160},{224,192},{256... | collective-permute-start | bytes 196616 | tf_op jit(solution)/shard_map/ppermute | solution.py:19
  90.7 7.5 %collective-permute-start.18 = (f32[4,1,32,128]{3,2,1,0:T(8,128)S(1)}, f32[4,1,32,128]{3,2,1,0:T(8,128)S(1)}, u32[]{:S(2)}, u32[]{:S(2)}) collective-permute-start(f32[4,1,32,128]{3,2,1,0:T(8,128)S(1)} %get-tuple-element.70), channel_id=1, source_target_pairs={{0,32},{32,64},{64,96},{96,128},{128,160},{160,192},{192,224},{224... | collective-permute-start | bytes 196616 | tf_op jit(solution)/shard_map/ppermute | solution.py:16
  98.3 5.9 %collective-permute-start.19 = (f32[4,7,1,128]{3,0,2,1:T(4,128)S(1)}, f32[4,7,1,128]{3,0,2,1:T(4,128)S(1)}, u32[]{:S(2)}, u32[]{:S(2)}) collective-permute-start(f32[4,7,1,128]{3,0,2,1:T(4,128)S(1)} %copy.495), channel_id=1, source_target_pairs={{4,0},{8,4},{12,8},{16,12},{20,16},{24,20},{28,24},{5,1},{9,5},{13... | collective-permute-start | bytes 43016 | tf_op jit(solution)/shard_map/ppermute | solution.py:19
  99.6 5.4 collective-permute-start.20
  105.6 7.0 %collective-permute-start.21 = (f32[4,7,34,1]{2,0,3,1:T(4,128)S(1)}, f32[4,7,34,1]{2,0,3,1:T(4,128)S(1)}, u32[]{:S(2)}, u32[]{:S(2)}) collective-permute-start(f32[4,7,34,1]{2,0,3,1:T(4,128)S(1)} %copy.501), channel_id=1, source_target_pairs={{1,0},{2,1},{3,2},{5,4},{6,5},{7,6},{9,8},{10,9},{11,10},{13,12},{... | collective-permute-start | bytes 11432 | tf_op jit(solution)/shard_map/ppermute | solution.py:19
  107.2 5.8 %collective-permute-start.22 = (f32[4,7,34,1]{2,0,3,1:T(4,128)S(1)}, f32[4,7,34,1]{2,0,3,1:T(4,128)S(1)}, u32[]{:S(2)}, u32[]{:S(2)}) collective-permute-start(f32[4,7,34,1]{2,0,3,1:T(4,128)S(1)} %copy.503), channel_id=1, source_target_pairs={{0,1},{1,2},{2,3},{4,5},{5,6},{6,7},{8,9},{9,10},{10,11},{12,13},{... | collective-permute-start | bytes 11432 | tf_op jit(solution)/shard_map/ppermute | solution.py:16
  115.3 7.5 %collective-permute-start.23 = (f32[4,1,32,128]{3,2,1,0:T(8,128)S(1)}, f32[4,1,32,128]{3,2,1,0:T(8,128)S(1)}, u32[]{:S(2)}, u32[]{:S(2)}) collective-permute-start(f32[4,1,32,128]{3,2,1,0:T(8,128)S(1)} %get-tuple-element.69), channel_id=1, source_target_pairs={{32,0},{64,32},{96,64},{128,96},{160,128},{192,160},{224,192},{256... | collective-permute-start | bytes 196616 | tf_op jit(solution)/shard_map/ppermute | solution.py:19
  117.3 6.9 %collective-permute-start.24 = (f32[4,1,32,128]{3,2,1,0:T(8,128)S(1)}, f32[4,1,32,128]{3,2,1,0:T(8,128)S(1)}, u32[]{:S(2)}, u32[]{:S(2)}) collective-permute-start(f32[4,1,32,128]{3,2,1,0:T(8,128)S(1)} %get-tuple-element.68), channel_id=1, source_target_pairs={{0,32},{32,64},{64,96},{96,128},{128,160},{160,192},{192,224},{224... | collective-permute-start | bytes 196616 | tf_op jit(solution)/shard_map/ppermute | solution.py:16
  124.2 5.9 %collective-permute-start.25 = (f32[4,7,1,128]{3,0,2,1:T(4,128)S(1)}, f32[4,7,1,128]{3,0,2,1:T(4,128)S(1)}, u32[]{:S(2)}, u32[]{:S(2)}) collective-permute-start(f32[4,7,1,128]{3,0,2,1:T(4,128)S(1)} %copy.505), channel_id=1, source_target_pairs={{4,0},{8,4},{12,8},{16,12},{20,16},{24,20},{28,24},{5,1},{9,5},{13... | collective-permute-start | bytes 43016 | tf_op jit(solution)/shard_map/ppermute | solution.py:19
  125.5 5.4 collective-permute-start.26
  131.5 6.1 %collective-permute-start.27 = (f32[4,7,34,1]{2,0,3,1:T(4,128)S(1)}, f32[4,7,34,1]{2,0,3,1:T(4,128)S(1)}, u32[]{:S(2)}, u32[]{:S(2)}) collective-permute-start(f32[4,7,34,1]{2,0,3,1:T(4,128)S(1)} %copy.511), channel_id=1, source_target_pairs={{1,0},{2,1},{3,2},{5,4},{6,5},{7,6},{9,8},{10,9},{11,10},{13,12},{... | collective-permute-start | bytes 11432 | tf_op jit(solution)/shard_map/ppermute | solution.py:19
  133.1 5.4 collective-permute-start.28
  139.3 7.9 %collective-permute-start.29 = (f32[4,1,32,128]{3,2,1,0:T(8,128)S(1)}, f32[4,1,32,128]{3,2,1,0:T(8,128)S(1)}, u32[]{:S(2)}, u32[]{:S(2)}) collective-permute-start(f32[4,1,32,128]{3,2,1,0:T(8,128)S(1)} %get-tuple-element.63), channel_id=1, source_target_pairs={{32,0},{64,32},{96,64},{128,96},{160,128},{192,160},{224,192},{256... | collective-permute-start | bytes 196616 | tf_op jit(solution)/shard_map/ppermute | solution.py:19
  141.2 7.3 %collective-permute-start.30 = (f32[4,1,32,128]{3,2,1,0:T(8,128)S(1)}, f32[4,1,32,128]{3,2,1,0:T(8,128)S(1)}, u32[]{:S(2)}, u32[]{:S(2)}) collective-permute-start(f32[4,1,32,128]{3,2,1,0:T(8,128)S(1)} %get-tuple-element.62), channel_id=1, source_target_pairs={{0,32},{32,64},{64,96},{96,128},{128,160},{160,192},{192,224},{224... | collective-permute-start | bytes 196616 | tf_op jit(solution)/shard_map/ppermute | solution.py:16
  148.6 7.5 %collective-permute-start.31 = (f32[4,7,1,128]{3,0,2,1:T(4,128)S(1)}, f32[4,7,1,128]{3,0,2,1:T(4,128)S(1)}, u32[]{:S(2)}, u32[]{:S(2)}) collective-permute-start(f32[4,7,1,128]{3,0,2,1:T(4,128)S(1)} %copy.515), channel_id=1, source_target_pairs={{4,0},{8,4},{12,8},{16,12},{20,16},{24,20},{28,24},{5,1},{9,5},{13... | collective-permute-start | bytes 43016 | tf_op jit(solution)/shard_map/ppermute | solution.py:19
  149.9 6.3 %collective-permute-start.32 = (f32[4,7,1,128]{3,0,2,1:T(4,128)S(1)}, f32[4,7,1,128]{3,0,2,1:T(4,128)S(1)}, u32[]{:S(2)}, u32[]{:S(2)}) collective-permute-start(f32[4,7,1,128]{3,0,2,1:T(4,128)S(1)} %copy.517), channel_id=1, source_target_pairs={{0,4},{4,8},{8,12},{12,16},{16,20},{20,24},{24,28},{1,5},{5,9},{9,... | collective-permute-start | bytes 43016 | tf_op jit(solution)/shard_map/ppermute | solution.py:16
  156.8 11.5 %collective-permute-start.33 = (f32[4,7,34,1]{2,0,3,1:T(4,128)S(1)}, f32[4,7,34,1]{2,0,3,1:T(4,128)}, u32[]{:S(2)}, u32[]{:S(2)}) collective-permute-start(f32[4,7,34,1]{2,0,3,1:T(4,128)S(1)} %copy.521), channel_id=1, source_target_pairs={{1,0},{2,1},{3,2},{5,4},{6,5},{7,6},{9,8},{10,9},{11,10},{13,12},{... | collective-permute-start | bytes 11432 | tf_op jit(solution)/shard_map/ppermute | solution.py:19
  159.0 10.4 %collective-permute-start.34 = (f32[4,7,34,1]{2,0,3,1:T(4,128)}, f32[4,7,34,1]{2,0,3,1:T(4,128)}, u32[]{:S(2)}, u32[]{:S(2)}) collective-permute-start(f32[4,7,34,1]{2,0,3,1:T(4,128)} %copy.523), channel_id=1, source_target_pairs={{0,1},{1,2},{2,3},{4,5},{5,6},{6,7},{8,9},{9,10},{10,11},{12,13},{... | collective-permute-start | bytes 11432 | tf_op jit(solution)/shard_map/ppermute | solution.py:16
  (29 other events, 672.9 us)
where the time goes:
time: 546 us; the launch traced here: 542 us
  other arithmetic  195 us (36%)
  blocking collectives  116 us (21%)
  starting transfers between devices  110 us (20%)
  local copies, waits for them, and re-layouts  62.4 us (11%)
  between operations  29.3 us (5%)
  matrix products  20.1 us (4%)
  waiting for transfers between devices  8.15 us (1%)
    div x2, other arithmetic, back_solve(): answer[i] = partial_sum / triangle[i, i]  123 us
    psum x1, blocking collectives, local(): gram = lax.psum(local_gram, ('gx', 'gy', 'gz'))  116 us
    ppermute x18, starting transfers between devices, padded(): lax.ppermute(lax.slice_in_dim(block, block.shape[dim] - width, None, axis...  81.2 us
    ppermute x17, starting transfers between devices, padded(): lax.ppermute(lax.slice_in_dim(block, 0, width, axis=dim), axis, backward)  28.9 us
    another operation x1, other arithmetic, back_solve(): return jnp.stack(answer)  19.3 us
    dot_general x20, matrix products, reflect_rows(): project = jnp.dot(tall, vector, precision=lax.Precision.HIGHEST) / weight  15.7 us
    reduce_sum x20, other arithmetic, reflect_rows(): length = jnp.sqrt(jnp.sum(column * column))  13.6 us
    reduce_sum x20, other arithmetic, reflect_rows(): weight = jnp.sum(vector * vector)  12 us
  transfers between devices with their start and end apart: 35, of which 8 were waited for; matrix products, arithmetic and copies ran while one was open for 6% of the time, Pallas kernels for 0%

commit v1 on v0

--- a/solution.py
+++ b/solution.py
@@ -89,7 +89,7 @@
         blocks.append((stencil(widened, coef_ext) - basis_shift * before) / basis_scale)
     tall = jnp.stack(blocks).reshape(len(blocks) * nrhs, -1)
     local_gram = jnp.dot(tall, tall.T, precision=lax.Precision.HIGHEST)
-    gram = lax.psum(local_gram, ("gx", "gy", "gz"))
+    gram = lax.psum(lax.psum(local_gram, ("gy", "gz")), "gx")
     upper = jnp.linalg.cholesky(gram).T
     weights = least_squares(upper, nrhs)
     kept = tall.shape[0] - nrhs

time: 546 us -> 633 us (1.16)
  blocking collectives: 116 us -> 201 us
    psum x1 -> x2, blocking collectives: 116 us -> 201 us  [local(): gram = lax.psum(lax.psum(local_gram, ('gy', 'gz')), 'gx')]
  transfers between devices with their start and end apart: 35 -> 35, of which waited for: 8 -> 8; matrix products, arithmetic and copies ran while one was open for 6% -> 5% of each run, Pallas kernels for 0% -> 0%
where the time goes in v1:
time: 633 us; the launch traced here: 626 us
  blocking collectives  201 us (32%)
  other arithmetic  195 us (31%)
  starting transfers between devices  110 us (17%)
  local copies, waits for them, and re-layouts  62.4 us (10%)
  between operations  29.3 us (5%)
  matrix products  20.1 us (3%)
  waiting for transfers between devices  8.15 us (1%)
    psum x2, blocking collectives, local(): gram = lax.psum(lax.psum(local_gram, ('gy', 'gz')), 'gx')  201 us
    div x2, other arithmetic, back_solve(): answer[i] = partial_sum / triangle[i, i]  123 us
    ppermute x18, starting transfers between devices, padded(): lax.ppermute(lax.slice_in_dim(block, block.shape[dim] - width, None, axis...  81.2 us
    ppermute x17, starting transfers between devices, padded(): lax.ppermute(lax.slice_in_dim(block, 0, width, axis=dim), axis, backward)  28.9 us
    another operation x1, other arithmetic, back_solve(): return jnp.stack(answer)  19.3 us
    dot_general x20, matrix products, reflect_rows(): project = jnp.dot(tall, vector, precision=lax.Precision.HIGHEST) / weight  15.7 us
    reduce_sum x20, other arithmetic, reflect_rows(): length = jnp.sqrt(jnp.sum(column * column))  13.6 us
  transfers between devices with their start and end apart: 35, of which 8 were waited for; matrix products, arithmetic and copies ran while one was open for 5% of the time, Pallas kernels for 0%

profile of v1, /device:TPU:1, one launch (start us, length us, event | category | flops | bytes accessed | tf_op | source)
XLA Modules:
  0.0 625.6 jit_solution(4169096291923980434)
XLA Ops:
  0.9 5.5 collective-permute-start.1
  6.5 4.7 collective-permute-start.4
  12.1 1.9 collective-permute-start.2
  14.0 2.4 collective-permute-start
  24.1 5.2 collective-permute-start.6
  31.2 2.0 copy.479
  33.2 1.9 copy.481
  36.0 3.1 collective-permute-start.9
  45.9 4.0 collective-permute-start.10
  50.8 2.4 fusion.42
  56.7 2.2 constant_dynamic-update-slice_fusion.9
  58.9 1.9 collective-permute-start.11
  60.8 5.3 collective-permute-start.12
  68.8 4.0 collective-permute-start.14
  78.9 4.0 collective-permute-start.16
  90.7 6.2 collective-permute-start.18
  99.6 4.5 collective-permute-start.20
  107.2 4.5 collective-permute-start.22
  117.3 5.6 collective-permute-start.24
  125.5 4.5 collective-permute-start.26
  133.1 4.5 collective-permute-start.28
  139.3 1.9 collective-permute-start.29
  141.2 6.0 collective-permute-start.30
  149.9 5.5 collective-permute-start.32
  159.0 5.1 collective-permute-start.34
  171.2 2.2 fusion.49
  175.2 2.1 fusion.311
  177.3 121.5 %psum.14 = f32[20,20]{0,1:T(8,128)S(1)} all-reduce(f32[20,20]{0,1:T(8,128)S(1)} %fusion.311), channel_id=1, replica_groups=mesh['gx'=16,'gy'=8,'gz'=4] {'gy','gz'}, use_global_device_ids=true, to_apply=%region_0.0 | all-reduce | flops 400 | bytes 3200 | tf_op jit(solution)/shard_map/psum | solution.py:92
  298.8 79.0 %psum.15 = f32[20,20]{0,1:T(8,128)S(1)} all-reduce(f32[20,20]{0,1:T(8,128)S(1)} %psum.14), channel_id=1, replica_groups=mesh['gx'=16,'gy'=8,'gz'=4] {'gx'}, use_global_device_ids=true, to_apply=%region_1.0 | all-reduce | flops 400 | bytes 3200 | tf_op jit(solution)/shard_map/psum | solution.py:92
  479.1 65.5 %subtract_divide_fusion = (f32[1,4]{1,0:T(1,128)S(1)}, f32[1,4]{1,0:T(1,128)S(1)}, f32[1,4]{1,0:T(1,128)S(1)}, f32[1,4]{1,0:T(1,128)S(1)}, f32[1,4]{1,0:T(1,128)...) fusion(f32[20,20]{1,0:T(8,128)S(1)} %multiply_select_fusion, ...), kind=kLoop, calls=%fused_computation.602 | loop fusion | flops 784 | bytes 884 | tf_op jit(solution)/shard_map/div | solution.py:61
  545.0 57.8 %fusion.191 = (f32[4]{0:T(128)S(1)}, f32[4]{0:T(128)S(1)}, f32[4]{0:T(128)S(1)}, f32[4]{0:T(128)S(1)}, f32[4]{0:T(128)S(1)}, /*index=5*/f32[4]{0:T(128)S(1)}, f3...) fusion(f32[20,20]{1,0:T(8,128)S(1)} %multiply_select_fusion, f32[1,4]{1,0:T(1,128)S(1)} %get-tuple-element.16, ...), kind=kLoop, calls=%fused_computation.504 | loop fusion | flops 704 | bytes 756 | tf_op jit(solution)/shard_map/div | solution.py:61
  602.8 19.3 %fusion.244 = (f32[1,4]{1,0:T(1,128)S(1)}, f32[4]{0:T(128)S(1)}) fusion(f32[1,4]{1,0:T(1,128)S(1)} %get-tuple-element.19, f32[1,4]{1,0:T(1,128)S(1)} %get-tuple-element.18, f32[1,4]{1,0:T(1,128)S(1)} %get-tuple-element.17, f32[1,4]{1,0:T(1,128)S(1)} %get-tuple-element.16, f32[4]{0:T(128)S(1)} %get-tuple-element.31, f32[4]{0:T(128)S(1)} %get-tuple-element.30, ...), kind=kLoop, calls=%fused_computation.656 | loop fusion | flops 240 | bytes 412 | tf_op jit(solution)/shard_map/stack | solution.py:62
  (371 shorter events, 149.8 us)
Async XLA Ops:
  0.9 15.5 %collective-permute-start.1 = (f32[4,1,32,128]{3,2,1,0:T(8,128)S(1)}, f32[4,1,32,128]{3,2,1,0:T(8,128)S(1)}, u32[]{:S(2)}, u32[]{:S(2)}) collective-permute-start(f32[4,1,32,128]{3,2,1,0:T(8,128)S(1)} %get-tuple-element.80), channel_id=1, source_target_pairs={{0,32},{32,64},{64,96},{96,128},{128,160},{160,192},{192,224},{224... | collective-permute-start | bytes 196616 | tf_op jit(solution)/shard_map/ppermute | solution.py:16
  6.5 11.0 %collective-permute-start.4 = (f32[4,1,32,128]{3,2,1,0:T(8,128)S(1)}, f32[4,1,32,128]{3,2,1,0:T(8,128)S(1)}, u32[]{:S(2)}, u32[]{:S(2)}) collective-permute-start(f32[4,1,32,128]{3,2,1,0:T(8,128)S(1)} %get-tuple-element.79), channel_id=1, source_target_pairs={{32,0},{64,32},{96,64},{128,96},{160,128},{192,160},{224,192},{256... | collective-permute-start | bytes 196616 | tf_op jit(solution)/shard_map/ppermute | solution.py:19
  12.1 9.3 %collective-permute-start.2 = (f32[4,1,32,128]{3,2,1,0:T(8,128)S(1)}, f32[4,1,32,128]{3,2,1,0:T(8,128)S(1)}, u32[]{:S(2)}, u32[]{:S(2)}) collective-permute-start(f32[4,1,32,128]{3,2,1,0:T(8,128)S(1)} %get-tuple-element.82), channel_id=1, source_target_pairs={{0,32},{32,64},{64,96},{96,128},{128,160},{160,192},{192,224},{224... | collective-permute-start | bytes 196616 | tf_op jit(solution)/shard_map/ppermute | solution.py:16
  14.0 7.5 %collective-permute-start = (f32[4,1,32,128]{3,2,1,0:T(8,128)S(1)}, f32[4,1,32,128]{3,2,1,0:T(8,128)S(1)}, u32[]{:S(2)}, u32[]{:S(2)}) collective-permute-start(f32[4,1,32,128]{3,2,1,0:T(8,128)S(1)} %get-tuple-element.81), channel_id=1, source_target_pairs={{32,0},{64,32},{96,64},{128,96},{160,128},{192,160},{224,192},{256... | collective-permute-start | bytes 196616 | tf_op jit(solution)/shard_map/ppermute | solution.py:19
  18.4 12.8 %collective-permute-start.5 = (f32[4,7,1,128]{3,1,2,0:T(8,128)}, f32[4,7,1,128]{3,1,2,0:T(8,128)S(1)}, u32[]{:S(2)}, u32[]{:S(2)}) collective-permute-start(f32[4,7,1,128]{3,1,2,0:T(8,128)} %get-tuple-element.50), channel_id=1, source_target_pairs={{0,4},{4,8},{8,12},{12,16},{16,20},{20,24},{24,28},{1,5},{5,9},{9,... | collective-permute-start | bytes 43016 | tf_op jit(solution)/shard_map/ppermute | solution.py:16
  20.1 13.1 %collective-permute-start.8 = (f32[4,7,1,128]{3,1,2,0:T(8,128)}, f32[4,7,1,128]{3,1,2,0:T(8,128)S(1)}, u32[]{:S(2)}, u32[]{:S(2)}) collective-permute-start(f32[4,7,1,128]{3,1,2,0:T(8,128)} %get-tuple-element.51), channel_id=1, source_target_pairs={{4,0},{8,4},{12,8},{16,12},{20,16},{24,20},{28,24},{5,1},{9,5},{13... | collective-permute-start | bytes 43016 | tf_op jit(solution)/shard_map/ppermute | solution.py:19
  22.2 16.9 %collective-permute-start.3 = (f32[4,7,1,128]{3,0,2,1:T(4,128)}, f32[4,7,1,128]{3,0,2,1:T(4,128)}, u32[]{:S(2)}, u32[]{:S(2)}) collective-permute-start(f32[4,7,1,128]{3,0,2,1:T(4,128)} %copy.550), channel_id=1, source_target_pairs={{4,0},{8,4},{12,8},{16,12},{20,16},{24,20},{28,24},{5,1},{9,5},{13... | collective-permute-start | bytes 43016 | tf_op jit(solution)/shard_map/ppermute | solution.py:19
  24.1 15.8 %collective-permute-start.6 = (f32[4,7,1,128]{3,0,2,1:T(4,128)}, f32[4,7,1,128]{3,0,2,1:T(4,128)}, u32[]{:S(2)}, u32[]{:S(2)}) collective-permute-start(f32[4,7,1,128]{3,0,2,1:T(4,128)} %copy.551), channel_id=1, source_target_pairs={{0,4},{4,8},{8,12},{12,16},{16,20},{20,24},{24,28},{1,5},{5,9},{9,... | collective-permute-start | bytes 43016 | tf_op jit(solution)/shard_map/ppermute | solution.py:16
  36.0 14.8 %collective-permute-start.9 = (f32[4,7,34,1]{2,1,3,0:T(8,128)S(1)}, f32[4,7,34,1]{2,1,3,0:T(8,128)S(1)}, u32[]{:S(2)}, u32[]{:S(2)}) collective-permute-start(f32[4,7,34,1]{2,1,3,0:T(8,128)S(1)} %pad_maximum_fusion.93), channel_id=1, source_target_pairs={{0,1},{1,2},{2,3},{4,5},{5,6},{6,7},{8,9},{9,10},{10,11},{12,13},{... | collective-permute-start | bytes 11432 | tf_op jit(solution)/shard_map/ppermute | solution.py:16
  43.2 11.2 %collective-permute-start.7 = (f32[4,7,34,1]{2,0,3,1:T(4,128)S(1)}, f32[4,7,34,1]{2,0,3,1:T(4,128)S(1)}, u32[]{:S(2)}, u32[]{:S(2)}) collective-permute-start(f32[4,7,34,1]{2,0,3,1:T(4,128)S(1)} %copy.476), channel_id=1, source_target_pairs={{1,0},{2,1},{3,2},{5,4},{6,5},{7,6},{9,8},{10,9},{11,10},{13,12},{... | collective-permute-start | bytes 11432 | tf_op jit(solution)/shard_map/ppermute | solution.py:19
  45.9 9.7 %collective-permute-start.10 = (f32[4,7,34,1]{2,0,3,1:T(4,128)S(1)}, f32[4,7,34,1]{2,0,3,1:T(4,128)S(1)}, u32[]{:S(2)}, u32[]{:S(2)}) collective-permute-start(f32[4,7,34,1]{2,0,3,1:T(4,128)S(1)} %copy.483), channel_id=1, source_target_pairs={{0,1},{1,2},{2,3},{4,5},{5,6},{6,7},{8,9},{9,10},{10,11},{12,13},{... | collective-permute-start | bytes 11432 | tf_op jit(solution)/shard_map/ppermute | solution.py:16
  58.9 7.3 %collective-permute-start.11 = (f32[4,1,32,128]{3,2,1,0:T(8,128)S(1)}, f32[4,1,32,128]{3,2,1,0:T(8,128)S(1)}, u32[]{:S(2)}, u32[]{:S(2)}) collective-permute-start(f32[4,1,32,128]{3,2,1,0:T(8,128)S(1)} %get-tuple-element.73), channel_id=1, source_target_pairs={{32,0},{64,32},{96,64},{128,96},{160,128},{192,160},{224,192},{256... | collective-permute-start | bytes 196616 | tf_op jit(solution)/shard_map/ppermute | solution.py:19
  60.8 6.6 %collective-permute-start.12 = (f32[4,1,32,128]{3,2,1,0:T(8,128)S(1)}, f32[4,1,32,128]{3,2,1,0:T(8,128)S(1)}, u32[]{:S(2)}, u32[]{:S(2)}) collective-permute-start(f32[4,1,32,128]{3,2,1,0:T(8,128)S(1)} %get-tuple-element.72), channel_id=1, source_target_pairs={{0,32},{32,64},{64,96},{96,128},{128,160},{160,192},{192,224},{224... | collective-permute-start | bytes 196616 | tf_op jit(solution)/shard_map/ppermute | solution.py:16
  76.2 6.6 %collective-permute-start.15 = (f32[4,7,34,1]{2,0,3,1:T(4,128)S(1)}, f32[4,7,34,1]{2,0,3,1:T(4,128)S(1)}, u32[]{:S(2)}, u32[]{:S(2)}) collective-permute-start(f32[4,7,34,1]{2,0,3,1:T(4,128)S(1)} %copy.491), channel_id=1, source_target_pairs={{1,0},{2,1},{3,2},{5,4},{6,5},{7,6},{9,8},{10,9},{11,10},{13,12},{... | collective-permute-start | bytes 11432 | tf_op jit(solution)/shard_map/ppermute | solution.py:19
  88.8 8.2 %collective-permute-start.17 = (f32[4,1,32,128]{3,2,1,0:T(8,128)S(1)}, f32[4,1,32,128]{3,2,1,0:T(8,128)S(1)}, u32[]{:S(2)}, u32[]{:S(2)}) collective-permute-start(f32[4,1,32,128]{3,2,1,0:T(8,128)S(1)} %get-tuple-element.71), channel_id=1, source_target_pairs={{32,0},{64,32},{96,64},{128,96},{160,128},{192,160},{224,192},{256... | collective-permute-start | bytes 196616 | tf_op jit(solution)/shard_map/ppermute | solution.py:19
  90.7 7.5 %collective-permute-start.18 = (f32[4,1,32,128]{3,2,1,0:T(8,128)S(1)}, f32[4,1,32,128]{3,2,1,0:T(8,128)S(1)}, u32[]{:S(2)}, u32[]{:S(2)}) collective-permute-start(f32[4,1,32,128]{3,2,1,0:T(8,128)S(1)} %get-tuple-element.70), channel_id=1, source_target_pairs={{0,32},{32,64},{64,96},{96,128},{128,160},{160,192},{192,224},{224... | collective-permute-start | bytes 196616 | tf_op jit(solution)/shard_map/ppermute | solution.py:16
  98.3 5.9 collective-permute-start.19
  99.6 5.4 collective-permute-start.20
  105.6 7.0 %collective-permute-start.21 = (f32[4,7,34,1]{2,0,3,1:T(4,128)S(1)}, f32[4,7,34,1]{2,0,3,1:T(4,128)S(1)}, u32[]{:S(2)}, u32[]{:S(2)}) collective-permute-start(f32[4,7,34,1]{2,0,3,1:T(4,128)S(1)} %copy.501), channel_id=1, source_target_pairs={{1,0},{2,1},{3,2},{5,4},{6,5},{7,6},{9,8},{10,9},{11,10},{13,12},{... | collective-permute-start | bytes 11432 | tf_op jit(solution)/shard_map/ppermute | solution.py:19
  107.2 5.8 collective-permute-start.22
  115.3 7.5 %collective-permute-start.23 = (f32[4,1,32,128]{3,2,1,0:T(8,128)S(1)}, f32[4,1,32,128]{3,2,1,0:T(8,128)S(1)}, u32[]{:S(2)}, u32[]{:S(2)}) collective-permute-start(f32[4,1,32,128]{3,2,1,0:T(8,128)S(1)} %get-tuple-element.69), channel_id=1, source_target_pairs={{32,0},{64,32},{96,64},{128,96},{160,128},{192,160},{224,192},{256... | collective-permute-start | bytes 196616 | tf_op jit(solution)/shard_map/ppermute | solution.py:19
  117.3 6.9 %collective-permute-start.24 = (f32[4,1,32,128]{3,2,1,0:T(8,128)S(1)}, f32[4,1,32,128]{3,2,1,0:T(8,128)S(1)}, u32[]{:S(2)}, u32[]{:S(2)}) collective-permute-start(f32[4,1,32,128]{3,2,1,0:T(8,128)S(1)} %get-tuple-element.68), channel_id=1, source_target_pairs={{0,32},{32,64},{64,96},{96,128},{128,160},{160,192},{192,224},{224... | collective-permute-start | bytes 196616 | tf_op jit(solution)/shard_map/ppermute | solution.py:16
  124.2 5.9 collective-permute-start.25
  125.5 5.4 collective-permute-start.26
  131.5 6.1 collective-permute-start.27
  133.1 5.4 collective-permute-start.28
  139.3 7.9 %collective-permute-start.29 = (f32[4,1,32,128]{3,2,1,0:T(8,128)S(1)}, f32[4,1,32,128]{3,2,1,0:T(8,128)S(1)}, u32[]{:S(2)}, u32[]{:S(2)}) collective-permute-start(f32[4,1,32,128]{3,2,1,0:T(8,128)S(1)} %get-tuple-element.63), channel_id=1, source_target_pairs={{32,0},{64,32},{96,64},{128,96},{160,128},{192,160},{224,192},{256... | collective-permute-start | bytes 196616 | tf_op jit(solution)/shard_map/ppermute | solution.py:19
  141.2 7.3 %collective-permute-start.30 = (f32[4,1,32,128]{3,2,1,0:T(8,128)S(1)}, f32[4,1,32,128]{3,2,1,0:T(8,128)S(1)}, u32[]{:S(2)}, u32[]{:S(2)}) collective-permute-start(f32[4,1,32,128]{3,2,1,0:T(8,128)S(1)} %get-tuple-element.62), channel_id=1, source_target_pairs={{0,32},{32,64},{64,96},{96,128},{128,160},{160,192},{192,224},{224... | collective-permute-start | bytes 196616 | tf_op jit(solution)/shard_map/ppermute | solution.py:16
  148.6 7.5 %collective-permute-start.31 = (f32[4,7,1,128]{3,0,2,1:T(4,128)S(1)}, f32[4,7,1,128]{3,0,2,1:T(4,128)S(1)}, u32[]{:S(2)}, u32[]{:S(2)}) collective-permute-start(f32[4,7,1,128]{3,0,2,1:T(4,128)S(1)} %copy.515), channel_id=1, source_target_pairs={{4,0},{8,4},{12,8},{16,12},{20,16},{24,20},{28,24},{5,1},{9,5},{13... | collective-permute-start | bytes 43016 | tf_op jit(solution)/shard_map/ppermute | solution.py:19
  149.9 6.3 %collective-permute-start.32 = (f32[4,7,1,128]{3,0,2,1:T(4,128)S(1)}, f32[4,7,1,128]{3,0,2,1:T(4,128)S(1)}, u32[]{:S(2)}, u32[]{:S(2)}) collective-permute-start(f32[4,7,1,128]{3,0,2,1:T(4,128)S(1)} %copy.517), channel_id=1, source_target_pairs={{0,4},{4,8},{8,12},{12,16},{16,20},{20,24},{24,28},{1,5},{5,9},{9,... | collective-permute-start | bytes 43016 | tf_op jit(solution)/shard_map/ppermute | solution.py:16
  156.8 11.5 %collective-permute-start.33 = (f32[4,7,34,1]{2,0,3,1:T(4,128)S(1)}, f32[4,7,34,1]{2,0,3,1:T(4,128)}, u32[]{:S(2)}, u32[]{:S(2)}) collective-permute-start(f32[4,7,34,1]{2,0,3,1:T(4,128)S(1)} %copy.521), channel_id=1, source_target_pairs={{1,0},{2,1},{3,2},{5,4},{6,5},{7,6},{9,8},{10,9},{11,10},{13,12},{... | collective-permute-start | bytes 11432 | tf_op jit(solution)/shard_map/ppermute | solution.py:19
  159.0 10.4 %collective-permute-start.34 = (f32[4,7,34,1]{2,0,3,1:T(4,128)}, f32[4,7,34,1]{2,0,3,1:T(4,128)}, u32[]{:S(2)}, u32[]{:S(2)}) collective-permute-start(f32[4,7,34,1]{2,0,3,1:T(4,128)} %copy.523), channel_id=1, source_target_pairs={{0,1},{1,2},{2,3},{4,5},{5,6},{6,7},{8,9},{9,10},{10,11},{12,13},{... | collective-permute-start | bytes 11432 | tf_op jit(solution)/shard_map/ppermute | solution.py:16
  (29 other events, 672.9 us)
